TPU v7x, 32 devices: a whole 2x2x4 slice. The times are simulated.
32 devices in a mesh: batch: 4 (over y, x), seq: 8 (over z, core).
Axes of the slice: x: 2, y: 2, z: 4, core: 2. Of those that a mesh axis runs over, the one named last changes fastest.
Arguments:
- query_source: bfloat16 [4, 2816, 4096], P('batch', 'seq'), may hold values from -6 to 6
- key_source: bfloat16 [4, 2816, 4096], P('batch', 'seq'), may hold values from -6 to 6
- value_source: bfloat16 [4, 2816, 4096], P('batch', 'seq'), may hold values from -6 to 6
- send_list: int32 [4, 8, 4, 32], P('batch', 'seq'), may hold values from 0 to 351, as said below
- slab_from: int32 [4, 2048], P('batch', 'seq'), may hold values from 0 to 479, as said below
- bounds: int32 [4, 16], P('batch'), may hold values from 0 to 1920, as said below
- filters: bfloat16 [4096, 128], replicated, may hold values from -0.5 to 0.5
- skip_gain: float32 [4096], replicated, may hold values from 0.5 to 2
- out_cotangent: bfloat16 [4, 2048, 4096], P('batch', 'seq'), may hold values from -6 to 6
Outputs:
- gated_output: bfloat16 [4, 2048, 4096], P('batch', 'seq')
- query_grad: bfloat16 [4, 2816, 4096], P('batch', 'seq')
- key_grad: bfloat16 [4, 2816, 4096], P('batch', 'seq')
- value_grad: bfloat16 [4, 2816, 4096], P('batch', 'seq')
- filter_grad: float32 [4096, 128], P('seq')
- skip_grad: float32 [4096], P('seq')
Inputs may be any that keep to these rules, and one draw needn't show every extreme that they name: For source (e, s) and destination batch index d, the first n entries of send_list[e, s, d] are distinct source rows of (e, s) that go to (d, s), with n between 0 and 32, n = 0 for d = e, and n = 32 for some pair at every s; the remaining entries are 0. No source row is listed twice, and no listed row is also kept by its own device. `slab_from`: the 256 entries of one device name, in no set order, its kept own source rows (values below 352) and every row listed to it: value 352 + e * 32 + m for the m-th listed row from source e; each exactly once. bounds[b, 0] = 0 and the starts rise by 128 or more; the last is at most 1920.
All inputs are finite; a program needn't handle non-finite values.
Results may differ from a plain program's by a relative error of at most 0.0075.
Values may be sent and summed in bfloat16 or wider, within the bound.
A program may use at most 192 MiB of HBM per device.

v0:
```python
import functools

import jax
import jax.numpy as jnp
import numpy as np
from jax import lax
from jax.experimental import pallas as pl
from jax.experimental.pallas import tpu as pltpu
from jax.sharding import PartitionSpec as P

CHANNELS = 4096
TAPS = 128
SPAN = 128
MOVE = 32
ROWS = 256
WINDOW = 2 * SPAN
EXTRA = 8
GROUPS = 2

F32 = jnp.float32
BF16 = jnp.bfloat16


def waves(places):
    angles = 2.0 * np.pi / WINDOW * np.outer(np.arange(SPAN) + 0.5, places)
    return np.cos(angles), np.sin(angles)


def forward_waves(places):
    cos, sin = waves(places)
    return np.concatenate([cos, -sin], axis=0).astype(np.float32)


def inverse_waves(places):
    cos, sin = waves(places)
    return (np.concatenate([cos, -sin], axis=0).T / SPAN).astype(np.float32)


def dot(a, b):
    return jnp.dot(a, b, preferred_element_type=F32)


def times(a, b):
    return (a.astype(F32) * b.astype(F32)).astype(BF16)


def pack_kernel(routes, query, key, value, sent):
    batches = sent.shape[0]
    width = sent.shape[2]
    picked_query = dot(routes[...], query[...]).astype(BF16)
    picked_mixed = dot(routes[...], times(key[...], value[...])).astype(BF16)
    sent[:, :MOVE, :] = picked_query.reshape(batches, MOVE, width)
    sent[:, MOVE:, :] = picked_mixed.reshape(batches, MOVE, width)


def slab_kernel(own_hot, far_hot, query, key, value, arrived, cotangent, query_slab, right, left):
    width = query.shape[1]
    far_query = arrived[:, :MOVE, :].reshape(-1, width)
    far_mixed = arrived[:, MOVE:, :].reshape(-1, width)
    queries = (dot(own_hot[...], query[...]) + dot(far_hot[...], far_query)).astype(BF16)
    mixed = (
        dot(own_hot[...], times(key[...], value[...])) + dot(far_hot[...], far_mixed)
    ).astype(BF16)
    gated = times(cotangent[...], queries)
    query_slab[...] = queries
    right[:SPAN, :] = mixed[:SPAN]
    right[SPAN:, :] = gated[SPAN:]
    left[:SPAN, :] = mixed[SPAN:]
    left[SPAN:, :] = gated[:SPAN]


def main_kernel(
    flag,
    wave_in,
    wave_gate,
    wave_ahead,
    wave_taps,
    wave_out,
    wave_grad,
    wave_weights,
    far_back,
    filters,
    skip_gain,
    query_slab,
    right,
    left,
    from_left,
    from_right,
    cotangent,
    *rest,
):
    out, grad_query, grad_mixed, sent, sums = rest[-5:]
    width = query_slab.shape[1]
    batches = sent.shape[0]
    last = flag[0] == 1
    taps = lax.dot_general(
        wave_taps[...], filters[...], (((1,), (1,)), ((), ())), preferred_element_type=F32
    )
    tap_re, tap_im = taps[:SPAN], taps[SPAN:]
    gain = skip_gain[...]
    mixed = (right[:SPAN, :], left[:SPAN, :])
    gated = (left[SPAN:, :], right[SPAN:, :])
    before = (from_left[:SPAN, :], jnp.where(last, mixed[0], from_right[:SPAN, :]))
    ahead = (jnp.where(last, gated[1], from_right[SPAN:, :]), from_left[SPAN:, :])
    weight_re = jnp.zeros((SPAN, width), F32)
    weight_im = jnp.zeros((SPAN, width), F32)
    skip_sum = jnp.zeros((1, width), F32)
    query_parts, mixed_parts = [], []
    for block in range(2):
        rows = slice(block * SPAN, (block + 1) * SPAN)
        spec = dot(wave_in[block], jnp.concatenate([before[block], mixed[block]], axis=0))
        gate = dot(wave_gate[block], gated[block])
        both = gate + dot(wave_ahead[block], ahead[block])
        prods, backs = [], []
        for parity in range(2):
            re = slice(2 * parity * SPAN, (2 * parity + 1) * SPAN)
            im = slice((2 * parity + 1) * SPAN, (2 * parity + 2) * SPAN)
            x_re, x_im = spec[re], spec[im]
            g_re, g_im = gate[re], gate[im]
            b_re, b_im = both[re], both[im]
            prods += [
                (tap_re * x_re - tap_im * x_im).astype(BF16),
                (tap_re * x_im + tap_im * x_re).astype(BF16),
            ]
            backs += [
                (tap_re * b_re + tap_im * b_im).astype(BF16),
                (tap_re * b_im - tap_im * b_re).astype(BF16),
            ]
            weight_re += g_re * x_re + g_im * x_im
            weight_im += g_re * x_im - g_im * x_re
        mixed_float = mixed[block].astype(F32)
        gated_float = gated[block].astype(F32)
        filtered = dot(wave_out[block], jnp.concatenate(prods, axis=0)) + gain * mixed_float
        back = dot(wave_grad[block], jnp.concatenate(backs, axis=0)) + gain * gated_float
        out[rows, :] = (query_slab[rows, :].astype(F32) * filtered).astype(BF16)
        query_parts.append((cotangent[rows, :].astype(F32) * filtered).astype(BF16))
        mixed_parts.append(back.astype(BF16))
        grad_query[rows, :] = query_parts[-1]
        grad_mixed[rows, :] = mixed_parts[-1]
        skip_sum += jnp.sum(gated_float * mixed_float, axis=0, keepdims=True)
    far_query = dot(far_back[...], jnp.concatenate(query_parts, axis=0)).astype(BF16)
    far_mixed = dot(far_back[...], jnp.concatenate(mixed_parts, axis=0)).astype(BF16)
    sent[:, :MOVE, :] = far_query.reshape(batches, MOVE, width)
    sent[:, MOVE:, :] = far_mixed.reshape(batches, MOVE, width)
    weights = jnp.concatenate([weight_re, weight_im], axis=0)
    sums[:TAPS, :] = dot(wave_weights[...], weights.astype(BF16))
    sums[TAPS:, :] = jnp.broadcast_to(skip_sum, (EXTRA, width))


def settle_kernel(own_back, routes_back, slab_query, slab_mixed, arrived, key, value, *rest):
    query_grad, key_grad, value_grad = rest[-3:]
    width = key.shape[1]
    far_query = arrived[:, :MOVE, :].reshape(-1, width)
    far_mixed = arrived[:, MOVE:, :].reshape(-1, width)
    query_grad[...] = (
        dot(own_back[...], slab_query[...]) + dot(routes_back[...], far_query)
    ).astype(BF16)
    mixed = dot(own_back[...], slab_mixed[...]) + dot(routes_back[...], far_mixed)
    key_grad[...] = (mixed * value[...].astype(F32)).astype(BF16)
    value_grad[...] = (mixed * key[...].astype(F32)).astype(BF16)


def whole(shape):
    return pl.BlockSpec(shape, lambda i: (0,) * len(shape))


def cost(flops, moved):
    return pl.CostEstimate(flops=int(flops), bytes_accessed=int(moved), transcendentals=0)


def params():
    return pltpu.CompilerParams(vmem_limit_bytes=40 * 1024 * 1024)


def on_device(
    query_source,
    key_source,
    value_source,
    send_list,
    slab_from,
    bounds,
    filters,
    skip_gain,
    out_cotangent,
):
    shards = lax.axis_size("seq")
    batches = lax.axis_size("batch")
    shard_index = lax.axis_index("seq")
    query = query_source[0]
    key = key_source[0]
    value = value_source[0]
    cotangent = out_cotangent[0]
    routes = send_list[0, 0].reshape(-1)
    picks = slab_from[0]
    starts = bounds[0]
    source_rows = query.shape[0]
    far_rows = batches * MOVE
    length = shards * ROWS
    piece = CHANNELS // shards
    width = min(256, piece)
    splits = piece // width
    steps = shards // GROUPS
    part = steps * width

    own_ids = jnp.arange(source_rows, dtype=jnp.int32)
    far_ids = source_rows + jnp.arange(far_rows, dtype=jnp.int32)
    routes_hot = (routes[:, None] == own_ids[None, :]).astype(BF16)
    routes_back = (own_ids[:, None] == routes[None, :]).astype(BF16)
    own_hot = (picks[:, None] == own_ids[None, :]).astype(BF16)
    far_hot = (picks[:, None] == far_ids[None, :]).astype(BF16)
    own_back = (own_ids[:, None] == picks[None, :]).astype(BF16)
    far_back = (far_ids[:, None] == picks[None, :]).astype(BF16)

    span_ids = jnp.stack([shard_index, 2 * shards - 1 - shard_index])
    places = (span_ids[:, None] - 1) * SPAN + jnp.arange(3 * SPAN, dtype=jnp.int32)[None, :]
    counted = jnp.sum((starts[None, None, :] <= places[:, :, None]).astype(jnp.int32), axis=2)
    inside = (places >= 0) & (places < length)
    parity = (counted - 1) % 2
    masks = jnp.stack(
        [(inside & (parity == 0)), (inside & (parity == 1))], axis=1
    ).astype(F32)

    def masked_in(matrix, mask):
        return (matrix[None, None] * mask[:, :, None, :]).reshape(2, 4 * SPAN, -1).astype(BF16)

    def masked_out(matrix, mask):
        wide = matrix[None, :, None, :] * jnp.swapaxes(mask, 1, 2)[:, :, :, None]
        return wide.reshape(2, SPAN, 4 * SPAN).astype(BF16)

    near, far = np.arange(SPAN), SPAN + np.arange(SPAN)
    wave_in = masked_in(forward_waves(np.arange(WINDOW)), masks[:, :, :WINDOW])
    wave_gate = masked_in(forward_waves(near), masks[:, :, SPAN:WINDOW])
    wave_ahead = masked_in(forward_waves(far), masks[:, :, WINDOW:])
    wave_taps = jnp.asarray(forward_waves(near), BF16)
    wave_out = masked_out(inverse_waves(far), masks[:, :, SPAN:WINDOW])
    wave_grad = masked_out(inverse_waves(near), masks[:, :, SPAN:WINDOW])
    wave_weights = jnp.asarray(inverse_waves(SPAN - np.arange(TAPS)), BF16)
    flag = (shard_index == shards - 1).astype(jnp.int32).reshape(1)
    gain = skip_gain.reshape(1, CHANNELS)

    def place(split, group):
        return lambda i: (group * steps + i) * splits + split

    chunks = [(split, group) for split in range(splits) for group in range(GROUPS)]
    right_way = [(i, i + 1) for i in range(shards - 1)]
    left_way = [(i + 1, i) for i in range(shards - 1)]

    def part_spec(rows):
        return pl.BlockSpec((rows, width), lambda i: (0, i))

    sent_spec = pl.BlockSpec((batches, 2 * MOVE, width), lambda i: (0, 0, i))
    sent_shape = jax.ShapeDtypeStruct((batches, 2 * MOVE, part), BF16)
    slab_shape = jax.ShapeDtypeStruct((ROWS, part), BF16)
    any_spec = pl.BlockSpec(memory_space=pl.ANY)

    arrived = {}
    for chunk in chunks:
        at = place(*chunk)
        full = lambda rows: pl.BlockSpec((rows, width), lambda i: (0, at(i)))
        sent = pl.pallas_call(
            pack_kernel,
            grid=(steps,),
            in_specs=[whole((far_rows, source_rows))] + [full(source_rows)] * 3,
            out_specs=sent_spec,
            out_shape=sent_shape,
            compiler_params=params(),
            cost_estimate=cost(4 * far_rows * source_rows * part, 8 * source_rows * part),
        )(routes_hot, query, key, value)
        arrived[chunk] = lax.all_to_all(sent, "batch", split_axis=0, concat_axis=0, tiled=True)

    slabs = {}
    for chunk in chunks:
        at = place(*chunk)
        full = lambda rows: pl.BlockSpec((rows, width), lambda i: (0, at(i)))
        query_slab, right, left = pl.pallas_call(
            slab_kernel,
            grid=(steps,),
            in_specs=[whole((ROWS, source_rows)), whole((ROWS, far_rows))]
            + [full(source_rows)] * 3
            + [sent_spec, full(ROWS)],
            out_specs=[part_spec(ROWS)] * 3,
            out_shape=[slab_shape] * 3,
            compiler_params=params(),
            cost_estimate=cost(4 * ROWS * 480 * part, 12 * source_rows * part),
        )(own_hot, far_hot, query, key, value, arrived[chunk], cotangent)
        from_left = lax.ppermute(right, "seq", right_way)
        from_right = lax.ppermute(left, "seq", left_way)
        slabs[chunk] = (query_slab, right, left, from_left, from_right)

    out = None
    grads = {}
    for chunk in chunks:
        at = place(*chunk)
        full = lambda rows: pl.BlockSpec((rows, width), lambda i: (0, at(i)))
        carried = [] if out is None else [out]
        operands = [
            flag,
            wave_in,
            wave_gate,
            wave_ahead,
            wave_taps,
            wave_out,
            wave_grad,
            wave_weights,
            far_back,
        ]
        in_specs = [pl.BlockSpec(memory_space=pltpu.SMEM)]
        in_specs += [whole(operand.shape) for operand in operands[1:]]
        in_specs += [
            pl.BlockSpec((width, TAPS), lambda i: (at(i), 0)),
            full(1),
        ]
        in_specs += [part_spec(ROWS)] * 5 + [full(ROWS)]
        operands += [filters, gain, *slabs[chunk], cotangent]
        aliases = {len(operands): 0} if carried else {}
        out, slab_query, slab_mixed, sent, sums = pl.pallas_call(
            main_kernel,
            grid=(steps,),
            in_specs=in_specs + [any_spec] * len(carried),
            out_specs=[full(ROWS), part_spec(ROWS), part_spec(ROWS), sent_spec, part_spec(TAPS + EXTRA)],
            out_shape=[
                jax.ShapeDtypeStruct((ROWS, CHANNELS), BF16),
                slab_shape,
                slab_shape,
                sent_shape,
                jax.ShapeDtypeStruct((TAPS + EXTRA, part), F32),
            ],
            input_output_aliases=aliases,
            compiler_params=params(),
            cost_estimate=cost(3000 * 1024 * part, 30 * ROWS * part),
        )(*operands, *carried)
        back = lax.all_to_all(sent, "batch", split_axis=0, concat_axis=0, tiled=True)
        grads[chunk] = (slab_query, slab_mixed, back, sums)

    totals = []
    for split in range(splits):
        joined = jnp.concatenate([grads[split, group][3] for group in range(GROUPS)], axis=1)
        shared = lax.psum_scatter(joined, "seq", scatter_dimension=1, tiled=True)
        totals.append(lax.psum(shared, "batch"))
    total = jnp.concatenate(totals, axis=1)

    results = []
    for chunk in chunks:
        at = place(*chunk)
        full = lambda rows: pl.BlockSpec((rows, width), lambda i: (0, at(i)))
        operands = [own_back, routes_back, *grads[chunk][:3], key, value]
        results = pl.pallas_call(
            settle_kernel,
            grid=(steps,),
            in_specs=[whole((source_rows, ROWS)), whole((source_rows, far_rows))]
            + [part_spec(ROWS)] * 2
            + [sent_spec]
            + [full(source_rows)] * 2
            + [any_spec] * len(results),
            out_specs=[full(source_rows)] * 3,
            out_shape=[jax.ShapeDtypeStruct((source_rows, CHANNELS), BF16)] * 3,
            input_output_aliases={len(operands) + n: n for n in range(len(results))},
            compiler_params=params(),
            cost_estimate=cost(4 * 480 * ROWS * part, 14 * source_rows * part),
        )(*operands, *results)
    factor = float(batches * shards * ROWS) ** (-0.5)
    return (
        out[None],
        results[0][None],
        results[1][None],
        results[2][None],
        jnp.transpose(total[:TAPS]) * factor,
        total[TAPS] * factor,
    )


def solution(mesh):
    return jax.shard_map(
        on_device,
        mesh=mesh,
        in_specs=(
            P("batch", "seq", None),
            P("batch", "seq", None),
            P("batch", "seq", None),
            P("batch", "seq", None, None),
            P("batch", "seq"),
            P("batch", None),
            P(),
            P(),
            P("batch", "seq", None),
        ),
        out_specs=(
            P("batch", "seq", None),
            P("batch", "seq", None),
            P("batch", "seq", None),
            P("batch", "seq", None),
            P("seq", None),
            P("seq"),
        ),
        check_vma=False,
    )
```

profile of v0, /device:TPU:0, one launch (start us, length us, event | category | flops | bytes accessed | tf_op | source)
XLA Modules:
  0.0 277.3 jit_solution(7837523928296751093)
XLA Ops:
  16.1 5.2 %all-to-all-start.3 = ((bf16[4,64,1024]{2,1,0:T(8,128)(2,1)}), bf16[4,64,1024]{2,1,0:T(8,128)(2,1)S(1)}, u32[]{:S(2)}, u32[]{:S(2)}) async-start(bf16[4,64,1024]{2,1,0:T(8,128)(2,1)} %copy-done.30), calls=%async_computation.3 | async-start | bytes 1048576 | tf_op jit(solution)/shard_map/all_to_all | solution.py:269
  27.4 1.9 all-to-all-done.3.arrived
  30.1 3.5 %all-to-all-start.2 = ((bf16[4,64,1024]{2,1,0:T(8,128)(2,1)}), bf16[4,64,1024]{2,1,0:T(8,128)(2,1)S(1)}, u32[]{:S(2)}, u32[]{:S(2)}) async-start(bf16[4,64,1024]{2,1,0:T(8,128)(2,1)} %copy-done.31), calls=%async_computation.2 | async-start | bytes 1048576 | tf_op jit(solution)/shard_map/all_to_all | solution.py:269
  40.7 4.1 %all-to-all-start = ((bf16[4,64,1024]{2,1,0:T(8,128)(2,1)}), bf16[4,64,1024]{2,1,0:T(8,128)(2,1)}, u32[]{:S(2)}, u32[]{:S(2)}) async-start(bf16[4,64,1024]{2,1,0:T(8,128)(2,1)} %copy-done.27), calls=%async_computation | async-start | bytes 1048576 | tf_op jit(solution)/shard_map/all_to_all | solution.py:269
  49.7 2.0 mul.158
  51.7 2.3 mul.159
  60.0 3.0 %shard_map.206 = (bf16[256,1024]{1,0:T(8,128)(2,1)S(1)}, bf16[256,1024]{1,0:T(8,128)(2,1)}, bf16[256,1024]{1,0:T(8,128)(2,1)}) custom-call(bf16[256,352]{1,0:T(8,128)(2,1)S(1)} %fusion.3.own_hot, bf16[256,128]{1,0:T(8,128)(2,1)S(1)} %copy-done.32, bf16[352,4096]{1,0:T(8,128)(2,1)S(1)} %bitcast.72, bf16[352,4096]{1,0:T(8,128)(2,1)S(1)} %bitcast.48, ...), custom_call_target="tpu_custom_call" | custom-call | flops 503316480 | bytes 4325376 | tf_op jit(solution)/shard_map/pallas_call | solution.py:275
  63.8 2.2 collective-permute-start.6
  67.3 4.2 %all-to-all-start.1 = ((bf16[4,64,1024]{2,1,0:T(8,128)(2,1)}), bf16[4,64,1024]{2,1,0:T(8,128)(2,1)}, u32[]{:S(2)}, u32[]{:S(2)}) async-start(bf16[4,64,1024]{2,1,0:T(8,128)(2,1)} %copy-done.23), calls=%async_computation.1 | async-start | bytes 1048576 | tf_op jit(solution)/shard_map/all_to_all | solution.py:269
  71.5 2.1 multiply_convert_fusion
  81.8 3.0 %shard_map.204 = (bf16[256,1024]{1,0:T(8,128)(2,1)S(1)}, bf16[256,1024]{1,0:T(8,128)(2,1)}, bf16[256,1024]{1,0:T(8,128)(2,1)}) custom-call(bf16[256,352]{1,0:T(8,128)(2,1)S(1)} %fusion.3.own_hot, bf16[256,128]{1,0:T(8,128)(2,1)S(1)} %copy-done.33, bf16[352,4096]{1,0:T(8,128)(2,1)S(1)} %bitcast.73, bf16[352,4096]{1,0:T(8,128)(2,1)S(1)} %bitcast.49, ...), custom_call_target="tpu_custom_call" | custom-call | flops 503316480 | bytes 4325376 | tf_op jit(solution)/shard_map/pallas_call | solution.py:275
  84.8 4.9 %collective-permute-start.4 = (bf16[256,1024]{1,0:T(8,128)(2,1)}, bf16[256,1024]{1,0:T(8,128)(2,1)}, u32[]{:S(2)}, u32[]{:S(2)}) collective-permute-start(bf16[256,1024]{1,0:T(8,128)(2,1)} %get-tuple-element.57.right), channel_id=1, source_target_pairs={{0,1},{1,2},{2,3},{3,4},{4,5},{5,6},{6,7},{8,9},{9,10},{10,11},{11... | collective-permute-start | bytes 1572872 | tf_op jit(solution)/shard_map/ppermute | solution.py:286
  91.1 4.1 %shard_map.200 = (bf16[256,1024]{1,0:T(8,128)(2,1)S(1)}, bf16[256,1024]{1,0:T(8,128)(2,1)}, bf16[256,1024]{1,0:T(8,128)(2,1)S(1)}) custom-call(bf16[256,352]{1,0:T(8,128)(2,1)S(1)} %fusion.3.own_hot, bf16[256,128]{1,0:T(8,128)(2,1)S(1)} %copy-done.33, bf16[352,4096]{1,0:T(8,128)(2,1)S(1)} %bitcast.74, bf16[352,4096]{1,0:T(8,128)(2,1)S(1)} %bitcast.50, ...), custom_call_target="tpu_custom_call" | custom-call | flops 503316480 | bytes 4325376 | tf_op jit(solution)/shard_map/pallas_call | solution.py:275
  96.7 4.3 %collective-permute-start = (bf16[256,1024]{1,0:T(8,128)(2,1)}, bf16[256,1024]{1,0:T(8,128)(2,1)}, u32[]{:S(2)}, u32[]{:S(2)}) collective-permute-start(bf16[256,1024]{1,0:T(8,128)(2,1)} %get-tuple-element.51.right), channel_id=1, source_target_pairs={{0,1},{1,2},{2,3},{3,4},{4,5},{5,6},{6,7},{8,9},{9,10},{10,11},{11... | collective-permute-start | bytes 1572872 | tf_op jit(solution)/shard_map/ppermute | solution.py:286
  101.0 1.8 copy-done.7
  106.4 3.5 %shard_map.202 = (bf16[256,1024]{1,0:T(8,128)(2,1)S(1)}, bf16[256,1024]{1,0:T(8,128)(2,1)S(1)}, bf16[256,1024]{1,0:T(8,128)(2,1)S(1)}) custom-call(bf16[256,352]{1,0:T(8,128)(2,1)S(1)} %fusion.3.own_hot, bf16[256,128]{1,0:T(8,128)(2,1)S(1)} %copy-done.33, bf16[352,4096]{1,0:T(8,128)(2,1)S(1)} %bitcast.75, bf16[352,4096]{1,0:T(8,128)(2,1)S(1)} %bitcast.51, ...), custom_call_target="tpu_custom_call" | custom-call | flops 503316480 | bytes 4325376 | tf_op jit(solution)/shard_map/pallas_call | solution.py:275
  109.9 2.9 %collective-permute-start.2 = (bf16[256,1024]{1,0:T(8,128)(2,1)S(1)}, bf16[256,1024]{1,0:T(8,128)(2,1)S(1)}, u32[]{:S(2)}, u32[]{:S(2)}) collective-permute-start(bf16[256,1024]{1,0:T(8,128)(2,1)S(1)} %get-tuple-element.54.right), channel_id=1, source_target_pairs={{0,1},{1,2},{2,3},{3,4},{4,5},{5,6},{6,7},{8,9},{9,10},{10,11},{11... | collective-permute-start | bytes 1572872 | tf_op jit(solution)/shard_map/ppermute | solution.py:286
  114.2 7.2 %shard_map.207 = (bf16[256,4096]{1,0:T(8,128)(2,1)}, bf16[256,1024]{1,0:T(8,128)(2,1)S(1)}, bf16[256,1024]{1,0:T(8,128)(2,1)S(1)}, bf16[4,64,1024]{2,1,0:T(8,128)(2,1)S(1)}, f32[136,1024]{1,0:T(8,128)S(1)}) custom-call(s32[1]{0:T(128)} %bitcast.flag, bf16[2,512,256]{2,1,0:T(8,128)(2,1)S(1)} %copy-done.51, bf16[2,512,128]{2,1,0:T(8,128)(2,1)S(1)} %copy-done.59, ...), custom_call_target="tpu_custom_call" | custom-call | flops 3145728000 | bytes 7864320 | tf_op jit(solution)/shard_map/pallas_call | solution.py:316
  124.4 7.1 %shard_map.208 = (bf16[256,4096]{1,0:T(8,128)(2,1)}, bf16[256,1024]{1,0:T(8,128)(2,1)S(1)}, bf16[256,1024]{1,0:T(8,128)(2,1)S(1)}, bf16[4,64,1024]{2,1,0:T(8,128)(2,1)S(1)}, f32[136,1024]{1,0:T(8,128)S(1)}) custom-call(s32[1]{0:T(128)} %bitcast.flag, bf16[2,512,256]{2,1,0:T(8,128)(2,1)S(1)} %copy-done.51, ...), custom_call_target="tpu_custom_call", output_to_operand_aliasing={{0}: (17, {})} | custom-call | flops 3145728000 | bytes 7864320 | tf_op jit(solution)/shard_map/pallas_call | solution.py:316
  134.7 6.4 %shard_map.209 = (bf16[256,4096]{1,0:T(8,128)(2,1)}, bf16[256,1024]{1,0:T(8,128)(2,1)S(1)}, bf16[256,1024]{1,0:T(8,128)(2,1)S(1)}, bf16[4,64,1024]{2,1,0:T(8,128)(2,1)S(1)}, f32[136,1024]{1,0:T(8,128)S(1)}) custom-call(s32[1]{0:T(128)} %bitcast.flag, bf16[2,512,256]{2,1,0:T(8,128)(2,1)S(1)} %copy-done.51, ...), custom_call_target="tpu_custom_call", output_to_operand_aliasing={{0}: (17, {})} | custom-call | flops 3145728000 | bytes 7864320 | tf_op jit(solution)/shard_map/pallas_call | solution.py:316
  142.7 7.4 %shard_map.210 = (bf16[256,4096]{1,0:T(8,128)(2,1)}, bf16[256,1024]{1,0:T(8,128)(2,1)S(1)}, bf16[256,1024]{1,0:T(8,128)(2,1)S(1)}, bf16[4,64,1024]{2,1,0:T(8,128)(2,1)}, f32[136,1024]{1,0:T(8,128)S(1)}) custom-call(s32[1]{0:T(128)} %bitcast.flag, bf16[2,512,256]{2,1,0:T(8,128)(2,1)S(1)} %copy-done.51, ...), custom_call_target="tpu_custom_call", output_to_operand_aliasing={{0}: (17, {})} | custom-call | flops 3145728000 | bytes 7864320 | tf_op jit(solution)/shard_map/pallas_call | solution.py:316
  152.8 2.1 pad_maximum_fusion
  155.0 13.1 %all_to_all.40.arrived = bf16[4,64,1024]{2,1,0:T(8,128)(2,1)} all-to-all(bf16[4,64,1024]{2,1,0:T(8,128)(2,1)} %copy-done.55), channel_id=1, replica_groups=mesh['batch'=4,'seq'=8] {'batch'}, dimensions={0} | all-to-all | bytes 1048576 | tf_op jit(solution)/shard_map/all_to_all | solution.py:332
  168.0 13.5 %all_to_all.41.arrived = bf16[4,64,1024]{2,1,0:T(8,128)(2,1)} all-to-all(bf16[4,64,1024]{2,1,0:T(8,128)(2,1)} %copy-done.54), channel_id=1, replica_groups=mesh['batch'=4,'seq'=8] {'batch'}, dimensions={0} | all-to-all | bytes 1048576 | tf_op jit(solution)/shard_map/all_to_all | solution.py:332
  181.5 12.7 %all_to_all.42.arrived = bf16[4,64,1024]{2,1,0:T(8,128)(2,1)} all-to-all(bf16[4,64,1024]{2,1,0:T(8,128)(2,1)S(1)} %copy-done.53), channel_id=1, replica_groups=mesh['batch'=4,'seq'=8] {'batch'}, dimensions={0} | all-to-all | bytes 1048576 | tf_op jit(solution)/shard_map/all_to_all | solution.py:332
  194.2 4.1 %all-to-all-start.4 = ((bf16[4,64,1024]{2,1,0:T(8,128)(2,1)}), bf16[4,64,1024]{2,1,0:T(8,128)(2,1)}, u32[]{:S(2)}, u32[]{:S(2)}) async-start(bf16[4,64,1024]{2,1,0:T(8,128)(2,1)} %get-tuple-element.68), calls=%async_computation.4 | async-start | bytes 1048576 | tf_op jit(solution)/shard_map/all_to_all | solution.py:332
  198.5 24.3 %reduce-scatter.3.cloned.1.call-done = f32[136,256]{1,0:T(8,128)} async-done(((f32[136,2048]{1,0:T(8,128)}), f32[136,256]{1,0:T(8,128)}) %reduce-scatter.3.cloned.1.call-update) | async-done | bytes 139280 | tf_op jit(solution)/shard_map/reduce_scatter | solution.py:338
  227.8 3.0 %shard_map.211 = (bf16[352,4096]{1,0:T(8,128)(2,1)}, bf16[352,4096]{1,0:T(8,128)(2,1)}, bf16[352,4096]{1,0:T(8,128)(2,1)}) custom-call(bf16[352,256]{1,0:T(8,128)(2,1)S(1)} %fusion.4.own_back, bf16[352,128]{1,0:T(8,128)(2,1)S(1)} %fusion.7.routes_back, bf16[256,1024]{1,0:T(8,128)(2,1)S(1)} %copy-done.36, bf16[256,1024]{1,0:T(8,128)(2,1)S(1)} %copy-done.38, ...), custom_call_target="tpu_custom_call" | custom-call | flops 503316480 | bytes 5046272 | tf_op jit(solution)/shard_map/pallas_call | solution.py:347
  230.9 3.0 %shard_map.212 = (bf16[352,4096]{1,0:T(8,128)(2,1)}, bf16[352,4096]{1,0:T(8,128)(2,1)}, bf16[352,4096]{1,0:T(8,128)(2,1)}) custom-call(bf16[352,256]{1,0:T(8,128)(2,1)S(1)} %fusion.4.own_back, bf16[352,128]{1,0:T(8,128)(2,1)S(1)} %fusion.7.routes_back, bf16[256,1024]{1,0:T(8,128)(2,1)S(1)} %copy-done.40, ...), custom_call_target="tpu_custom_call", output_to_operand_aliasing={{0}: (7, {}), {1}: (8, {}), {2}: (9, {})} | custom-call | flops 503316480 | bytes 5046272 | tf_op jit(solution)/shard_map/pallas_call | solution.py:347
  233.9 3.0 %shard_map.213 = (bf16[352,4096]{1,0:T(8,128)(2,1)}, bf16[352,4096]{1,0:T(8,128)(2,1)}, bf16[352,4096]{1,0:T(8,128)(2,1)}) custom-call(bf16[352,256]{1,0:T(8,128)(2,1)S(1)} %fusion.4.own_back, bf16[352,128]{1,0:T(8,128)(2,1)S(1)} %fusion.7.routes_back, bf16[256,1024]{1,0:T(8,128)(2,1)S(1)} %copy-done.44, ...), custom_call_target="tpu_custom_call", output_to_operand_aliasing={{0}: (7, {}), {1}: (8, {}), {2}: (9, {})} | custom-call | flops 503316480 | bytes 5046272 | tf_op jit(solution)/shard_map/pallas_call | solution.py:347
  240.9 4.2 %shard_map.214 = (bf16[352,4096]{1,0:T(8,128)(2,1)}, bf16[352,4096]{1,0:T(8,128)(2,1)}, bf16[352,4096]{1,0:T(8,128)(2,1)}) custom-call(bf16[352,256]{1,0:T(8,128)(2,1)S(1)} %fusion.4.own_back, bf16[352,128]{1,0:T(8,128)(2,1)S(1)} %fusion.7.routes_back, bf16[256,1024]{1,0:T(8,128)(2,1)S(1)} %copy-done.48, ...), custom_call_target="tpu_custom_call", output_to_operand_aliasing={{0}: (7, {}), {1}: (8, {}), {2}: (9, {})} | custom-call | flops 503316480 | bytes 5046272 | tf_op jit(solution)/shard_map/pallas_call | solution.py:347
  245.0 22.4 %all-reduce.3.cloned.1.call-done = (f32[136,256]{1,0:T(8,128)}, f32[136,256]{1,0:T(8,128)}) async-done(((f32[136,256]{1,0:T(8,128)}, f32[136,256]{1,0:T(8,128)}), (f32[136,256]{1,0:T(8,128)}, f32[136,256]{1,0:T(8,128)})) %all-reduce.3.cloned.1.call-update) | async-done | bytes 278544 | tf_op jit(solution)/shard_map/psum | solution.py:339
  (220 shorter events, 74.5 us)
Async XLA Ops:
  16.1 13.2 %all-to-all-start.3 = ((bf16[4,64,1024]{2,1,0:T(8,128)(2,1)}), bf16[4,64,1024]{2,1,0:T(8,128)(2,1)S(1)}, u32[]{:S(2)}, u32[]{:S(2)}) async-start(bf16[4,64,1024]{2,1,0:T(8,128)(2,1)} %copy-done.30), calls=%async_computation.3 | async-start | bytes 1048576 | tf_op jit(solution)/shard_map/all_to_all | solution.py:269
  30.1 10.6 %all-to-all-start.2 = ((bf16[4,64,1024]{2,1,0:T(8,128)(2,1)}), bf16[4,64,1024]{2,1,0:T(8,128)(2,1)S(1)}, u32[]{:S(2)}, u32[]{:S(2)}) async-start(bf16[4,64,1024]{2,1,0:T(8,128)(2,1)} %copy-done.31), calls=%async_computation.2 | async-start | bytes 1048576 | tf_op jit(solution)/shard_map/all_to_all | solution.py:269
  40.7 13.3 %copy-start.21 = (bf16[4,64,1024]{2,1,0:T(8,128)(2,1)}, bf16[4,64,1024]{2,1,0:T(8,128)(2,1)S(1)}, u32[]{:S(2)}) copy-start(bf16[4,64,1024]{2,1,0:T(8,128)(2,1)S(1)} %all-to-all-done.2.arrived) | copy-start | bytes 1572868
  40.7 26.6 %all-to-all-start = ((bf16[4,64,1024]{2,1,0:T(8,128)(2,1)}), bf16[4,64,1024]{2,1,0:T(8,128)(2,1)}, u32[]{:S(2)}, u32[]{:S(2)}) async-start(bf16[4,64,1024]{2,1,0:T(8,128)(2,1)} %copy-done.27), calls=%async_computation | async-start | bytes 1048576 | tf_op jit(solution)/shard_map/all_to_all | solution.py:269
  60.0 11.6 %copy-start.72 = (f32[16,8,2,256]{3,1,2,0:T(8,128)S(1)}, f32[16,8,2,256]{3,1,2,0:T(8,128)}, u32[]{:S(2)}) copy-start(f32[16,8,2,256]{3,1,2,0:T(8,128)} %copy.48) | copy-start | bytes 786436
  63.8 13.6 %copy-start.73 = (f32[256,128]{1,0:T(8,128)S(1)}, f32[256,128]{1,0:T(8,128)}, u32[]{:S(2)}) copy-start(f32[256,128]{1,0:T(8,128)} %constant.69) | copy-start | bytes 393220
  63.8 46.1 %collective-permute-start.6 = (bf16[256,1024]{1,0:T(8,128)(2,1)}, bf16[256,1024]{1,0:T(8,128)(2,1)}, u32[]{:S(2)}, u32[]{:S(2)}) collective-permute-start(bf16[256,1024]{1,0:T(8,128)(2,1)} %get-tuple-element.60.right), channel_id=1, source_target_pairs={{0,1},{1,2},{2,3},{3,4},{4,5},{5,6},{6,7},{8,9},{9,10},{10,11},{11... | collective-permute-start | bytes 1572872 | tf_op jit(solution)/shard_map/ppermute | solution.py:286
  66.0 46.8 %collective-permute-start.7 = (bf16[256,1024]{1,0:T(8,128)(2,1)}, bf16[256,1024]{1,0:T(8,128)(2,1)}, u32[]{:S(2)}, u32[]{:S(2)}) collective-permute-start(bf16[256,1024]{1,0:T(8,128)(2,1)} %get-tuple-element.61.left), channel_id=1, source_target_pairs={{1,0},{2,1},{3,2},{4,3},{5,4},{6,5},{7,6},{9,8},{10,9},{11,10},{12... | collective-permute-start | bytes 1572872 | tf_op jit(solution)/shard_map/ppermute | solution.py:287
  67.3 33.7 %all-to-all-start.1 = ((bf16[4,64,1024]{2,1,0:T(8,128)(2,1)}), bf16[4,64,1024]{2,1,0:T(8,128)(2,1)}, u32[]{:S(2)}, u32[]{:S(2)}) async-start(bf16[4,64,1024]{2,1,0:T(8,128)(2,1)} %copy-done.23), calls=%async_computation.1 | async-start | bytes 1048576 | tf_op jit(solution)/shard_map/all_to_all | solution.py:269
  71.5 127.0 %reduce-scatter.5.cloned.1.call-start = ((), (), s32[]{:S(2)}) async-start(), calls=%async_computation.11 | async-start | bytes 1253376 | tf_op jit(solution)/shard_map/reduce_scatter | solution.py:338
  81.8 9.2 %copy-start.78 = (s32[128]{0:T(128)S(1)}, s32[128]{0:T(128)}, u32[]{:S(2)}) copy-start(s32[128]{0:T(128)} %copy-done.77) | copy-start | bytes 1540
  81.8 9.3 %copy-start.18 = (bf16[1,256,4096]{2,1,0:T(8,128)(2,1)S(1)}, bf16[1,256,4096]{2,1,0:T(8,128)(2,1)}, u32[]{:S(2)}) copy-start(bf16[1,256,4096]{2,1,0:T(8,128)(2,1)} %param.24) | copy-start | bytes 6291460
  84.8 10.3 %copy-start.67 = (bf16[256,1024]{1,0:T(8,128)(2,1)}, bf16[256,1024]{1,0:T(8,128)(2,1)S(1)}, u32[]{:S(2)}) copy-start(bf16[256,1024]{1,0:T(8,128)(2,1)S(1)} %get-tuple-element.56.query_slab) | copy-start | bytes 1572868
  84.8 38.2 %collective-permute-start.4 = (bf16[256,1024]{1,0:T(8,128)(2,1)}, bf16[256,1024]{1,0:T(8,128)(2,1)}, u32[]{:S(2)}, u32[]{:S(2)}) collective-permute-start(bf16[256,1024]{1,0:T(8,128)(2,1)} %get-tuple-element.57.right), channel_id=1, source_target_pairs={{0,1},{1,2},{2,3},{3,4},{4,5},{5,6},{6,7},{8,9},{9,10},{10,11},{11... | collective-permute-start | bytes 1572872 | tf_op jit(solution)/shard_map/ppermute | solution.py:286
  89.7 34.7 %collective-permute-start.5 = (bf16[256,1024]{1,0:T(8,128)(2,1)}, bf16[256,1024]{1,0:T(8,128)(2,1)}, u32[]{:S(2)}, u32[]{:S(2)}) collective-permute-start(bf16[256,1024]{1,0:T(8,128)(2,1)} %get-tuple-element.58.left), channel_id=1, source_target_pairs={{1,0},{2,1},{3,2},{4,3},{5,4},{6,5},{7,6},{9,8},{10,9},{11,10},{12... | collective-permute-start | bytes 1572872 | tf_op jit(solution)/shard_map/ppermute | solution.py:287
  96.7 45.9 %collective-permute-start = (bf16[256,1024]{1,0:T(8,128)(2,1)}, bf16[256,1024]{1,0:T(8,128)(2,1)}, u32[]{:S(2)}, u32[]{:S(2)}) collective-permute-start(bf16[256,1024]{1,0:T(8,128)(2,1)} %get-tuple-element.51.right), channel_id=1, source_target_pairs={{0,1},{1,2},{2,3},{3,4},{4,5},{5,6},{6,7},{8,9},{9,10},{10,11},{11... | collective-permute-start | bytes 1572872 | tf_op jit(solution)/shard_map/ppermute | solution.py:286
  106.3 7.9 %copy-start.58 = (bf16[2,512,128]{2,1,0:T(8,128)(2,1)S(1)}, bf16[2,512,128]{2,1,0:T(8,128)(2,1)}, u32[]{:S(2)}) copy-start(bf16[2,512,128]{2,1,0:T(8,128)(2,1)} %get-tuple-element.121.wave_ahead) | copy-start | bytes 786436
  106.3 7.9 %copy-start.59 = (bf16[2,512,128]{2,1,0:T(8,128)(2,1)S(1)}, bf16[2,512,128]{2,1,0:T(8,128)(2,1)}, u32[]{:S(2)}) copy-start(bf16[2,512,128]{2,1,0:T(8,128)(2,1)} %get-tuple-element.122.wave_gate) | copy-start | bytes 786436
  106.3 7.9 %copy-start.60 = (bf16[4096,128]{1,0:T(8,128)(2,1)S(1)}, bf16[4096,128]{1,0:T(8,128)(2,1)}, u32[]{:S(2)}) copy-start(bf16[4096,128]{1,0:T(8,128)(2,1)} %filters.7) | copy-start | bytes 3145732
  106.3 7.9 %copy-start.62 = (bf16[256,1024]{1,0:T(8,128)(2,1)S(1)}, bf16[256,1024]{1,0:T(8,128)(2,1)}, u32[]{:S(2)}) copy-start(bf16[256,1024]{1,0:T(8,128)(2,1)} %copy-done.61) | copy-start | bytes 1572868
  109.9 24.8 %collective-permute-start.2 = (bf16[256,1024]{1,0:T(8,128)(2,1)S(1)}, bf16[256,1024]{1,0:T(8,128)(2,1)S(1)}, u32[]{:S(2)}, u32[]{:S(2)}) collective-permute-start(bf16[256,1024]{1,0:T(8,128)(2,1)S(1)} %get-tuple-element.54.right), channel_id=1, source_target_pairs={{0,1},{1,2},{2,3},{3,4},{4,5},{5,6},{6,7},{8,9},{9,10},{10,11},{11... | collective-permute-start | bytes 1572872 | tf_op jit(solution)/shard_map/ppermute | solution.py:286
  112.8 21.9 %collective-permute-start.3 = (bf16[256,1024]{1,0:T(8,128)(2,1)S(1)}, bf16[256,1024]{1,0:T(8,128)(2,1)S(1)}, u32[]{:S(2)}, u32[]{:S(2)}) collective-permute-start(bf16[256,1024]{1,0:T(8,128)(2,1)S(1)} %get-tuple-element.55.left), channel_id=1, source_target_pairs={{1,0},{2,1},{3,2},{4,3},{5,4},{6,5},{7,6},{9,8},{10,9},{11,10},{12... | collective-permute-start | bytes 1572872 | tf_op jit(solution)/shard_map/ppermute | solution.py:287
  114.2 8.8 %copy-start.66 = (bf16[256,1024]{1,0:T(8,128)(2,1)S(1)}, bf16[256,1024]{1,0:T(8,128)(2,1)}, u32[]{:S(2)}) copy-start(bf16[256,1024]{1,0:T(8,128)(2,1)} %copy-done.65) | copy-start | bytes 1572868
  114.2 10.1 %copy-start.68 = (bf16[256,1024]{1,0:T(8,128)(2,1)S(1)}, bf16[256,1024]{1,0:T(8,128)(2,1)}, u32[]{:S(2)}) copy-start(bf16[256,1024]{1,0:T(8,128)(2,1)} %copy-done.67) | copy-start | bytes 1572868
  123.0 8.4 %copy-start.52 = (bf16[4,64,1024]{2,1,0:T(8,128)(2,1)}, bf16[4,64,1024]{2,1,0:T(8,128)(2,1)S(1)}, u32[]{:S(2)}) copy-start(bf16[4,64,1024]{2,1,0:T(8,128)(2,1)S(1)} %get-tuple-element.77) | copy-start | bytes 1572868
  123.0 19.6 %collective-permute-start.1 = (bf16[256,1024]{1,0:T(8,128)(2,1)S(1)}, bf16[256,1024]{1,0:T(8,128)(2,1)S(1)}, u32[]{:S(2)}, u32[]{:S(2)}) collective-permute-start(bf16[256,1024]{1,0:T(8,128)(2,1)S(1)} %copy-done.66), channel_id=1, source_target_pairs={{1,0},{2,1},{3,2},{4,3},{5,4},{6,5},{7,6},{9,8},{10,9},{11,10},{12... | collective-permute-start | bytes 1572872 | tf_op jit(solution)/shard_map/ppermute | solution.py:287
  134.7 8.0 %copy-start.64 = (bf16[256,1024]{1,0:T(8,128)(2,1)S(1)}, bf16[256,1024]{1,0:T(8,128)(2,1)}, u32[]{:S(2)}) copy-start(bf16[256,1024]{1,0:T(8,128)(2,1)} %copy-done.63) | copy-start | bytes 1572868
  152.8 70.1 %reduce-scatter.3.cloned.1.call-start = ((), (), s32[]{:S(2)}) async-start(), calls=%async_computation.10 | async-start | bytes 1253376 | tf_op jit(solution)/shard_map/reduce_scatter | solution.py:338
  154.9 26.6 %copy-start.53 = (bf16[4,64,1024]{2,1,0:T(8,128)(2,1)S(1)}, bf16[4,64,1024]{2,1,0:T(8,128)(2,1)}, u32[]{:S(2)}) copy-start(bf16[4,64,1024]{2,1,0:T(8,128)(2,1)} %copy-done.52) | copy-start | bytes 1572868
  154.9 67.9 %copy-start.76 = (s32[128]{0:T(128)S(1)}, s32[128]{0:T(128)}, u32[]{:S(2)}) copy-start(s32[128]{0:T(128)} %copy-done.75) | copy-start | bytes 1540
  194.2 42.8 %all-to-all-start.4 = ((bf16[4,64,1024]{2,1,0:T(8,128)(2,1)}), bf16[4,64,1024]{2,1,0:T(8,128)(2,1)}, u32[]{:S(2)}, u32[]{:S(2)}) async-start(bf16[4,64,1024]{2,1,0:T(8,128)(2,1)} %get-tuple-element.68), calls=%async_computation.4 | async-start | bytes 1048576 | tf_op jit(solution)/shard_map/all_to_all | solution.py:332
  198.4 69.1 %all-reduce.3.cloned.1.call-start = ((), (), s32[]{:S(2)}) async-start(), calls=%async_computation.12 | async-start | bytes 557056 | tf_op jit(solution)/shard_map/psum | solution.py:339
  (64 other events, 166.9 us)
Sparse Core Ops, SparseCore 0:
  152.9 36.2 reduce-scatter.4
  192.1 30.6 reduce-scatter.2
  225.8 41.5 all-reduce.2
where the time goes:
time: 279 us; the launch traced here: 277 us
  local copies, waits for them, and re-layouts  64.3 us (23%)
  Pallas kernels  60.4 us (22%)
  waiting for transfers between devices  49.3 us (18%)
  starting transfers between devices  40.6 us (15%)
  blocking collectives  39.2 us (14%)
  between operations  14.4 us (5%)
  other arithmetic  9.06 us (3%)
    unnamed x164, local copies, waits for them, and re-layouts  52.1 us
    all_to_all x3, blocking collectives, on_device(): lax.all_to_all(sent, 'batch', split_axis=0, concat_axis=0, tiled=True)  39.2 us
    pallas_call x4, Pallas kernels, on_device(): pl.pallas_call(main_kernel, grid=(steps,), in_specs=in_specs + [any_spec]...  28 us
    reduce_scatter x2, waiting for transfers between devices, on_device(): shared = lax.psum_scatter(joined, 'seq', scatter_dimension=1, tiled=True)  24.4 us
    psum x1, waiting for transfers between devices, on_device(): totals.append(lax.psum(shared, 'batch'))  22.4 us
    all_to_all x5, starting transfers between devices, on_device(): lax.all_to_all(sent, 'batch', split_axis=0, concat_axis=0, tiled=True)  21.1 us
    ppermute x4, starting transfers between devices, on_device(): from_left = lax.ppermute(right, 'seq', right_way)  14.3 us
    pallas_call x4, Pallas kernels, on_device(): pl.pallas_call(slab_kernel, grid=(steps,), in_specs=[whole((ROWS, source_...  13.6 us
  transfers between devices with their start and end apart: 16, of which 4 were waited for; matrix products, arithmetic and copies ran while one was open for 7% of the time, Pallas kernels for 19%

commit v1 on v0

--- a/solution.py
+++ b/solution.py
@@ -15,7 +15,6 @@
 ROWS = 256
 WINDOW = 2 * SPAN
 EXTRA = 8
-GROUPS = 2
 
 F32 = jnp.float32
 BF16 = jnp.bfloat16
@@ -69,15 +68,38 @@
     left[SPAN:, :] = gated[:SPAN]
 
 
+def weights_kernel(flag, wave_in, wave_gate, wave_weights, right, left, from_left, from_right, sums):
+    width = right.shape[1]
+    last = flag[0] == 1
+    mixed = (right[:SPAN, :], left[:SPAN, :])
+    gated = (left[SPAN:, :], right[SPAN:, :])
+    before = (from_left[:SPAN, :], jnp.where(last, mixed[0], from_right[:SPAN, :]))
+    weight_re = jnp.zeros((SPAN, width), F32)
+    weight_im = jnp.zeros((SPAN, width), F32)
+    skip_sum = jnp.zeros((1, width), F32)
+    for block in range(2):
+        spec = dot(wave_in[block], jnp.concatenate([before[block], mixed[block]], axis=0))
+        gate = dot(wave_gate[block], gated[block])
+        for parity in range(2):
+            re = slice(2 * parity * SPAN, (2 * parity + 1) * SPAN)
+            im = slice((2 * parity + 1) * SPAN, (2 * parity + 2) * SPAN)
+            weight_re += gate[re] * spec[re] + gate[im] * spec[im]
+            weight_im += gate[re] * spec[im] - gate[im] * spec[re]
+        skip_sum += jnp.sum(
+            gated[block].astype(F32) * mixed[block].astype(F32), axis=0, keepdims=True
+        )
+    weights = jnp.concatenate([weight_re, weight_im], axis=0)
+    sums[:TAPS, :] = dot(wave_weights[...], weights.astype(BF16))
+    sums[TAPS:, :] = jnp.broadcast_to(skip_sum, (EXTRA, width))
+
+
 def main_kernel(
     flag,
     wave_in,
-    wave_gate,
-    wave_ahead,
+    wave_both,
     wave_taps,
     wave_out,
     wave_grad,
-    wave_weights,
     far_back,
     filters,
     skip_gain,
@@ -89,7 +111,7 @@
     cotangent,
     *rest,
 ):
-    out, grad_query, grad_mixed, sent, sums = rest[-5:]
+    out, grad_query, grad_mixed, sent = rest[-4:]
     width = query_slab.shape[1]
     batches = sent.shape[0]
     last = flag[0] == 1
@@ -102,21 +124,16 @@
     gated = (left[SPAN:, :], right[SPAN:, :])
     before = (from_left[:SPAN, :], jnp.where(last, mixed[0], from_right[:SPAN, :]))
     ahead = (jnp.where(last, gated[1], from_right[SPAN:, :]), from_left[SPAN:, :])
-    weight_re = jnp.zeros((SPAN, width), F32)
-    weight_im = jnp.zeros((SPAN, width), F32)
-    skip_sum = jnp.zeros((1, width), F32)
     query_parts, mixed_parts = [], []
     for block in range(2):
         rows = slice(block * SPAN, (block + 1) * SPAN)
         spec = dot(wave_in[block], jnp.concatenate([before[block], mixed[block]], axis=0))
-        gate = dot(wave_gate[block], gated[block])
-        both = gate + dot(wave_ahead[block], ahead[block])
+        both = dot(wave_both[block], jnp.concatenate([gated[block], ahead[block]], axis=0))
         prods, backs = [], []
         for parity in range(2):
             re = slice(2 * parity * SPAN, (2 * parity + 1) * SPAN)
             im = slice((2 * parity + 1) * SPAN, (2 * parity + 2) * SPAN)
             x_re, x_im = spec[re], spec[im]
-            g_re, g_im = gate[re], gate[im]
             b_re, b_im = both[re], both[im]
             prods += [
                 (tap_re * x_re - tap_im * x_im).astype(BF16),
@@ -126,8 +143,6 @@
                 (tap_re * b_re + tap_im * b_im).astype(BF16),
                 (tap_re * b_im - tap_im * b_re).astype(BF16),
             ]
-            weight_re += g_re * x_re + g_im * x_im
-            weight_im += g_re * x_im - g_im * x_re
         mixed_float = mixed[block].astype(F32)
         gated_float = gated[block].astype(F32)
         filtered = dot(wave_out[block], jnp.concatenate(prods, axis=0)) + gain * mixed_float
@@ -137,14 +152,10 @@
         mixed_parts.append(back.astype(BF16))
         grad_query[rows, :] = query_parts[-1]
         grad_mixed[rows, :] = mixed_parts[-1]
-        skip_sum += jnp.sum(gated_float * mixed_float, axis=0, keepdims=True)
     far_query = dot(far_back[...], jnp.concatenate(query_parts, axis=0)).astype(BF16)
     far_mixed = dot(far_back[...], jnp.concatenate(mixed_parts, axis=0)).astype(BF16)
     sent[:, :MOVE, :] = far_query.reshape(batches, MOVE, width)
     sent[:, MOVE:, :] = far_mixed.reshape(batches, MOVE, width)
-    weights = jnp.concatenate([weight_re, weight_im], axis=0)
-    sums[:TAPS, :] = dot(wave_weights[...], weights.astype(BF16))
-    sums[TAPS:, :] = jnp.broadcast_to(skip_sum, (EXTRA, width))
 
 
 def settle_kernel(own_back, routes_back, slab_query, slab_mixed, arrived, key, value, *rest):
@@ -169,7 +180,7 @@
 
 
 def params():
-    return pltpu.CompilerParams(vmem_limit_bytes=40 * 1024 * 1024)
+    return pltpu.CompilerParams(vmem_limit_bytes=60 * 1024 * 1024)
 
 
 def on_device(
@@ -197,10 +208,10 @@
     far_rows = batches * MOVE
     length = shards * ROWS
     piece = CHANNELS // shards
-    width = min(256, piece)
-    splits = piece // width
-    steps = shards // GROUPS
-    part = steps * width
+    width = 512
+    splits = 2
+    part = CHANNELS // splits
+    steps = part // width
 
     own_ids = jnp.arange(source_rows, dtype=jnp.int32)
     far_ids = source_rows + jnp.arange(far_rows, dtype=jnp.int32)
@@ -230,7 +241,7 @@
     near, far = np.arange(SPAN), SPAN + np.arange(SPAN)
     wave_in = masked_in(forward_waves(np.arange(WINDOW)), masks[:, :, :WINDOW])
     wave_gate = masked_in(forward_waves(near), masks[:, :, SPAN:WINDOW])
-    wave_ahead = masked_in(forward_waves(far), masks[:, :, WINDOW:])
+    wave_both = masked_in(forward_waves(np.arange(WINDOW)), masks[:, :, SPAN:])
     wave_taps = jnp.asarray(forward_waves(near), BF16)
     wave_out = masked_out(inverse_waves(far), masks[:, :, SPAN:WINDOW])
     wave_grad = masked_out(inverse_waves(near), masks[:, :, SPAN:WINDOW])
@@ -238,10 +249,10 @@
     flag = (shard_index == shards - 1).astype(jnp.int32).reshape(1)
     gain = skip_gain.reshape(1, CHANNELS)
 
-    def place(split, group):
-        return lambda i: (group * steps + i) * splits + split
-
-    chunks = [(split, group) for split in range(splits) for group in range(GROUPS)]
+    def place(split):
+        return lambda i: split * steps + i
+
+    chunks = list(range(splits))
     right_way = [(i, i + 1) for i in range(shards - 1)]
     left_way = [(i + 1, i) for i in range(shards - 1)]
 
@@ -255,7 +266,7 @@
 
     arrived = {}
     for chunk in chunks:
-        at = place(*chunk)
+        at = place(chunk)
         full = lambda rows: pl.BlockSpec((rows, width), lambda i: (0, at(i)))
         sent = pl.pallas_call(
             pack_kernel,
@@ -270,7 +281,7 @@
 
     slabs = {}
     for chunk in chunks:
-        at = place(*chunk)
+        at = place(chunk)
         full = lambda rows: pl.BlockSpec((rows, width), lambda i: (0, at(i)))
         query_slab, right, left = pl.pallas_call(
             slab_kernel,
@@ -287,21 +298,43 @@
         from_right = lax.ppermute(left, "seq", left_way)
         slabs[chunk] = (query_slab, right, left, from_left, from_right)
 
+    parts = []
+    for chunk in chunks:
+        operands = [flag, wave_in, wave_gate, wave_weights, *slabs[chunk][1:]]
+        parts.append(
+            pl.pallas_call(
+                weights_kernel,
+                grid=(steps,),
+                in_specs=[pl.BlockSpec(memory_space=pltpu.SMEM)]
+                + [whole(operand.shape) for operand in operands[1:4]]
+                + [part_spec(ROWS)] * 4,
+                out_specs=part_spec(TAPS + EXTRA),
+                out_shape=jax.ShapeDtypeStruct((TAPS + EXTRA, part), F32),
+                compiler_params=params(),
+                cost_estimate=cost(1500 * 1024 * part, 12 * ROWS * part),
+            )(*operands)
+        )
+    joined = jnp.concatenate(parts, axis=1).astype(BF16)
+    pieces = jnp.swapaxes(joined.reshape(-1, shards, piece), 0, 1)
+    met = lax.all_to_all(pieces, "seq", split_axis=0, concat_axis=0, tiled=True)
+    summed = jnp.sum(met.astype(F32), axis=0).astype(BF16)
+    copies = jnp.broadcast_to(summed[None], (batches, *summed.shape))
+    shared = lax.all_to_all(copies, "batch", split_axis=0, concat_axis=0, tiled=True)
+    total = jnp.sum(shared.astype(F32), axis=0)
+
     out = None
     grads = {}
     for chunk in chunks:
-        at = place(*chunk)
+        at = place(chunk)
         full = lambda rows: pl.BlockSpec((rows, width), lambda i: (0, at(i)))
         carried = [] if out is None else [out]
         operands = [
             flag,
             wave_in,
-            wave_gate,
-            wave_ahead,
+            wave_both,
             wave_taps,
             wave_out,
             wave_grad,
-            wave_weights,
             far_back,
         ]
         in_specs = [pl.BlockSpec(memory_space=pltpu.SMEM)]
@@ -313,35 +346,27 @@
         in_specs += [part_spec(ROWS)] * 5 + [full(ROWS)]
         operands += [filters, gain, *slabs[chunk], cotangent]
         aliases = {len(operands): 0} if carried else {}
-        out, slab_query, slab_mixed, sent, sums = pl.pallas_call(
+        out, slab_query, slab_mixed, sent = pl.pallas_call(
             main_kernel,
             grid=(steps,),
             in_specs=in_specs + [any_spec] * len(carried),
-            out_specs=[full(ROWS), part_spec(ROWS), part_spec(ROWS), sent_spec, part_spec(TAPS + EXTRA)],
+            out_specs=[full(ROWS), part_spec(ROWS), part_spec(ROWS), sent_spec],
             out_shape=[
                 jax.ShapeDtypeStruct((ROWS, CHANNELS), BF16),
                 slab_shape,
                 slab_shape,
                 sent_shape,
-                jax.ShapeDtypeStruct((TAPS + EXTRA, part), F32),
             ],
             input_output_aliases=aliases,
             compiler_params=params(),
             cost_estimate=cost(3000 * 1024 * part, 30 * ROWS * part),
         )(*operands, *carried)
         back = lax.all_to_all(sent, "batch", split_axis=0, concat_axis=0, tiled=True)
-        grads[chunk] = (slab_query, slab_mixed, back, sums)
-
-    totals = []
-    for split in range(splits):
-        joined = jnp.concatenate([grads[split, group][3] for group in range(GROUPS)], axis=1)
-        shared = lax.psum_scatter(joined, "seq", scatter_dimension=1, tiled=True)
-        totals.append(lax.psum(shared, "batch"))
-    total = jnp.concatenate(totals, axis=1)
+        grads[chunk] = (slab_query, slab_mixed, back)
 
     results = []
     for chunk in chunks:
-        at = place(*chunk)
+        at = place(chunk)
         full = lambda rows: pl.BlockSpec((rows, width), lambda i: (0, at(i)))
         operands = [own_back, routes_back, *grads[chunk][:3], key, value]
         results = pl.pallas_call(

time: 279 us -> 171 us (0.61)
  local copies, waits for them, and re-layouts: 64.3 us -> 5.79 us
  waiting for transfers between devices: 49.3 us -> 20.6 us
  between operations: 14.4 us -> 0.97 us
  starting transfers between devices: 40.6 us -> 29.3 us
  Pallas kernels: 60.4 us -> 66.6 us
  blocking collectives: 39.2 us -> 35.7 us
    unnamed x164 -> x25, local copies, waits for them, and re-layouts: 52.1 us -> 2.87 us
    reduce_scatter x2 -> x0, waiting for transfers between devices: 24.4 us -> none  [on_device(): shared = lax.psum_scatter(joined, 'seq', scatter_dimension=1, tiled=True)]
    psum x1 -> x0, waiting for transfers between devices: 22.4 us -> none  [on_device(): totals.append(lax.psum(shared, 'batch'))]
    all_to_all x5 -> x4, waiting for transfers between devices: 2.45 us -> 20.6 us  [on_device(): lax.all_to_all(sent, 'batch', split_axis=0, concat_axis=0, tiled=True)]
    pallas_call x0 -> x2, Pallas kernels: none -> 13.7 us  [on_device(): pl.pallas_call(weights_kernel, grid=(steps,), in_specs=[pl.BlockSpec(memo...]
    pallas_call x4 -> x2, Pallas kernels: 28 us -> 19 us  [on_device(): pl.pallas_call(main_kernel, grid=(steps,), in_specs=in_specs + [any_spec]...]
    ppermute x4 -> x2, starting transfers between devices: 14.3 us -> 6.39 us  [on_device(): from_left = lax.ppermute(right, 'seq', right_way)]
    mul x4, local copies, waits for them, and re-layouts: 6.27 us -> 0.94 us  [masked_out(): wide = matrix[None, :, None, :] * jnp.swapaxes(mask, 1, 2)[:, :, :, None]]
  transfers between devices with their start and end apart: 16 -> 9, of which waited for: 4 -> 2; matrix products, arithmetic and copies ran while one was open for 7% -> 6% of each run, Pallas kernels for 19% -> 31%
where the time goes in v1:
time: 171 us; the launch traced here: 170 us
  Pallas kernels  66.6 us (39%)
  blocking collectives  35.7 us (21%)
  starting transfers between devices  29.3 us (17%)
  waiting for transfers between devices  20.6 us (12%)
  other arithmetic  11.2 us (7%)
  local copies, waits for them, and re-layouts  5.79 us (3%)
    all_to_all x1, blocking collectives, on_device(): met = lax.all_to_all(pieces, 'seq', split_axis=0, concat_axis=0, tiled=True)  35.7 us
    all_to_all x4, waiting for transfers between devices, on_device(): lax.all_to_all(sent, 'batch', split_axis=0, concat_axis=0, tiled=True)  20.6 us
    pallas_call x2, Pallas kernels, on_device(): pl.pallas_call(main_kernel, grid=(steps,), in_specs=in_specs + [any_spec]...  19 us
    all_to_all x4, starting transfers between devices, on_device(): lax.all_to_all(sent, 'batch', split_axis=0, concat_axis=0, tiled=True)  16.9 us
    pallas_call x2, Pallas kernels, on_device(): pl.pallas_call(weights_kernel, grid=(steps,), in_specs=[pl.BlockSpec(memo...  13.7 us
    pallas_call x2, Pallas kernels, on_device(): pl.pallas_call(settle_kernel, grid=(steps,), in_specs=[whole((source_rows...  12.4 us
    pallas_call x2, Pallas kernels, on_device(): pl.pallas_call(slab_kernel, grid=(steps,), in_specs=[whole((ROWS, source_...  12.1 us
    pallas_call x2, Pallas kernels, on_device(): pl.pallas_call(pack_kernel, grid=(steps,), in_specs=[whole((far_rows, sou...  9.36 us
  transfers between devices with their start and end apart: 9, of which 2 were waited for; matrix products, arithmetic and copies ran while one was open for 6% of the time, Pallas kernels for 31%

profile of v1, /device:TPU:0, one launch (start us, length us, event | category | flops | bytes accessed | tf_op | source)
XLA Modules:
  0.0 170.1 jit_solution(6198707924495589391)
XLA Ops:
  0.6 0.8 eq.120
  2.1 4.7 %shard_map.201 = bf16[4,64,2048]{2,1,0:T(8,128)(2,1)} custom-call(bf16[128,352]{1,0:T(8,128)(2,1)} %fusion.6.routes, bf16[352,4096]{1,0:T(8,128)(2,1)} %bitcast.63, bf16[352,4096]{1,0:T(8,128)(2,1)} %bitcast.51, bf16[352,4096]{1,0:T(8,128)(2,1)} %bitcast.57), custom_call_target="tpu_custom_call" | custom-call | flops 369098752 | bytes 5767168 | tf_op jit(solution)/shard_map/pallas_call | solution.py:271
  6.8 5.2 %all-to-all-start.1 = ((bf16[4,64,2048]{2,1,0:T(8,128)(2,1)}), bf16[4,64,2048]{2,1,0:T(8,128)(2,1)S(1)}, u32[]{:S(2)}, u32[]{:S(2)}) async-start(bf16[4,64,2048]{2,1,0:T(8,128)(2,1)} %shard_map.201), calls=%async_computation.1 | async-start | bytes 2097152 | tf_op jit(solution)/shard_map/all_to_all | solution.py:280
  12.0 4.7 %shard_map.199 = bf16[4,64,2048]{2,1,0:T(8,128)(2,1)} custom-call(bf16[128,352]{1,0:T(8,128)(2,1)} %fusion.6.routes, bf16[352,4096]{1,0:T(8,128)(2,1)} %bitcast.64, bf16[352,4096]{1,0:T(8,128)(2,1)} %bitcast.52, bf16[352,4096]{1,0:T(8,128)(2,1)} %bitcast.58), custom_call_target="tpu_custom_call" | custom-call | flops 369098752 | bytes 5767168 | tf_op jit(solution)/shard_map/pallas_call | solution.py:271
  17.7 0.8 fusion.3.own_hot
  18.4 7.2 %all-to-all-done.1.arrived = bf16[4,64,2048]{2,1,0:T(8,128)(2,1)S(1)} async-done(((bf16[4,64,2048]{2,1,0:T(8,128)(2,1)}), bf16[4,64,2048]{2,1,0:T(8,128)(2,1)S(1)}, u32[]{:S(2)}, u32[]{:S(2)}) %all-to-all-start.1) | async-done | bytes 1048608 | tf_op jit(solution)/shard_map/all_to_all | solution.py:280
  25.6 3.5 %all-to-all-start = ((bf16[4,64,2048]{2,1,0:T(8,128)(2,1)}), bf16[4,64,2048]{2,1,0:T(8,128)(2,1)S(1)}, u32[]{:S(2)}, u32[]{:S(2)}) async-start(bf16[4,64,2048]{2,1,0:T(8,128)(2,1)} %shard_map.199), calls=%async_computation | async-start | bytes 2097152 | tf_op jit(solution)/shard_map/all_to_all | solution.py:280
  29.2 6.1 %shard_map.202 = (bf16[256,2048]{1,0:T(8,128)(2,1)}, bf16[256,2048]{1,0:T(8,128)(2,1)}, bf16[256,2048]{1,0:T(8,128)(2,1)}) custom-call(bf16[256,352]{1,0:T(8,128)(2,1)} %fusion.3.own_hot, bf16[256,128]{1,0:T(8,128)(2,1)} %compare_convert_fusion.far_hot, bf16[352,4096]{1,0:T(8,128)(2,1)} %bitcast.65, bf16[352,4096]{1,0:T(8,128)(2,1)} %bitcast.53, ...), custom_call_target="tpu_custom_call" | custom-call | flops 1006632960 | bytes 8650752 | tf_op jit(solution)/shard_map/pallas_call | solution.py:286
  35.4 2.4 %collective-permute-start.2 = (bf16[256,2048]{1,0:T(8,128)(2,1)}, bf16[256,2048]{1,0:T(8,128)(2,1)}, u32[]{:S(2)}, u32[]{:S(2)}) collective-permute-start(bf16[256,2048]{1,0:T(8,128)(2,1)} %get-tuple-element.30.right), channel_id=1, source_target_pairs={{0,1},{1,2},{2,3},{3,4},{4,5},{5,6},{6,7},{8,9},{9,10},{10,11},{11... | collective-permute-start | bytes 3145736 | tf_op jit(solution)/shard_map/ppermute | solution.py:297
  37.8 1.3 collective-permute-start.3
  41.2 1.3 fusion
  42.4 1.0 copy-done
  43.4 6.0 %shard_map.200 = (bf16[256,2048]{1,0:T(8,128)(2,1)}, bf16[256,2048]{1,0:T(8,128)(2,1)}, bf16[256,2048]{1,0:T(8,128)(2,1)}) custom-call(bf16[256,352]{1,0:T(8,128)(2,1)} %fusion.3.own_hot, bf16[256,128]{1,0:T(8,128)(2,1)} %compare_convert_fusion.far_hot, bf16[352,4096]{1,0:T(8,128)(2,1)} %bitcast.66, bf16[352,4096]{1,0:T(8,128)(2,1)} %bitcast.54, ...), custom_call_target="tpu_custom_call" | custom-call | flops 1006632960 | bytes 8650752 | tf_op jit(solution)/shard_map/pallas_call | solution.py:286
  49.4 4.0 %collective-permute-start = (bf16[256,2048]{1,0:T(8,128)(2,1)}, bf16[256,2048]{1,0:T(8,128)(2,1)S(1)}, u32[]{:S(2)}, u32[]{:S(2)}) collective-permute-start(bf16[256,2048]{1,0:T(8,128)(2,1)} %get-tuple-element.27.right), channel_id=1, source_target_pairs={{0,1},{1,2},{2,3},{3,4},{4,5},{5,6},{6,7},{8,9},{9,10},{10,11},{11... | collective-permute-start | bytes 3145736 | tf_op jit(solution)/shard_map/ppermute | solution.py:297
  53.4 1.3 collective-permute-start.1
  55.4 0.9 multiply_convert_fusion
  56.3 9.5 %shard_map.203 = (bf16[256,4096]{1,0:T(8,128)(2,1)}, bf16[256,2048]{1,0:T(8,128)(2,1)}, bf16[256,2048]{1,0:T(8,128)(2,1)}, bf16[4,64,2048]{2,1,0:T(8,128)(2,1)}) custom-call(s32[1]{0:T(128)} %bitcast.flag, bf16[2,512,256]{2,1,0:T(8,128)(2,1)} %get-tuple-element.55.wave_in, bf16[2,512,256]{2,1,0:T(8,128)(2,1)} %get-tuple-element.54.wave_both, ...), custom_call_target="tpu_custom_call" | custom-call | flops 6291456000 | bytes 15728640 | tf_op jit(solution)/shard_map/pallas_call | solution.py:349
  65.8 1.0 copy-done.10
  66.8 9.6 %shard_map.204 = (bf16[256,4096]{1,0:T(8,128)(2,1)}, bf16[256,2048]{1,0:T(8,128)(2,1)}, bf16[256,2048]{1,0:T(8,128)(2,1)}, bf16[4,64,2048]{2,1,0:T(8,128)(2,1)}) custom-call(s32[1]{0:T(128)} %bitcast.flag, bf16[2,512,256]{2,1,0:T(8,128)(2,1)} %get-tuple-element.55.wave_in, ...), custom_call_target="tpu_custom_call", output_to_operand_aliasing={{0}: (15, {})} | custom-call | flops 6291456000 | bytes 15728640 | tf_op jit(solution)/shard_map/pallas_call | solution.py:349
  76.3 4.2 %all-to-all-start.2 = ((bf16[4,64,2048]{2,1,0:T(8,128)(2,1)}), bf16[4,64,2048]{2,1,0:T(8,128)(2,1)S(1)}, u32[]{:S(2)}, u32[]{:S(2)}) async-start(bf16[4,64,2048]{2,1,0:T(8,128)(2,1)} %get-tuple-element.36), calls=%async_computation.2 | async-start | bytes 2097152 | tf_op jit(solution)/shard_map/all_to_all | solution.py:364
  80.5 6.8 %shard_map.208 = f32[136,2048]{1,0:T(8,128)} custom-call(s32[1]{0:T(128)} %bitcast.flag, bf16[2,512,256]{2,1,0:T(8,128)(2,1)} %get-tuple-element.55.wave_in, bf16[2,512,128]{2,1,0:T(8,128)(2,1)} %fusion.2.wave_gate, bf16[128,256]{1,0:T(8,128)(2,1)} %constant.60.clone.wave_weights, bf16[256,2048]{1,0:T(8,128)(2,1)} %get-tuple-element.27.right, ...), custom_call_target="tpu_custom_call" | custom-call | flops 3145728000 | bytes 6291456 | tf_op jit(solution)/shard_map/pallas_call | solution.py:305
  87.3 1.3 convert.11
  88.7 6.9 %shard_map.207 = f32[136,2048]{1,0:T(8,128)} custom-call(s32[1]{0:T(128)} %bitcast.flag, bf16[2,512,256]{2,1,0:T(8,128)(2,1)} %get-tuple-element.55.wave_in, bf16[2,512,128]{2,1,0:T(8,128)(2,1)} %fusion.2.wave_gate, bf16[128,256]{1,0:T(8,128)(2,1)} %constant.60.clone.wave_weights, bf16[256,2048]{1,0:T(8,128)(2,1)} %get-tuple-element.30.right, ...), custom_call_target="tpu_custom_call" | custom-call | flops 3145728000 | bytes 6291456 | tf_op jit(solution)/shard_map/pallas_call | solution.py:305
  95.5 1.3 convert.10
  97.1 35.7 %all_to_all.30 = bf16[8,136,512]{2,1,0:T(8,128)(2,1)S(1)} all-to-all(bf16[8,136,512]{2,1,0:T(8,128)(2,1)S(1)} %maximum_bitcast_fusion), channel_id=1, replica_groups=mesh['batch'=4,'seq'=8] {'seq'}, dimensions={0} | all-to-all | bytes 2228224 | tf_op jit(solution)/shard_map/all_to_all | solution.py:319
  132.7 4.0 %all-to-all-start.3 = ((bf16[4,64,2048]{2,1,0:T(8,128)(2,1)}), bf16[4,64,2048]{2,1,0:T(8,128)(2,1)S(1)}, u32[]{:S(2)}, u32[]{:S(2)}) async-start(bf16[4,64,2048]{2,1,0:T(8,128)(2,1)} %get-tuple-element.39), calls=%async_computation.3 | async-start | bytes 2097152 | tf_op jit(solution)/shard_map/all_to_all | solution.py:364
  136.9 13.4 %all-to-all-done.3.arrived = bf16[4,64,2048]{2,1,0:T(8,128)(2,1)S(1)} async-done(((bf16[4,64,2048]{2,1,0:T(8,128)(2,1)}), bf16[4,64,2048]{2,1,0:T(8,128)(2,1)S(1)}, u32[]{:S(2)}, u32[]{:S(2)}) %all-to-all-start.3) | async-done | bytes 1048608 | tf_op jit(solution)/shard_map/all_to_all | solution.py:364
  150.3 0.9 broadcast_in_dim.14
  151.3 3.5 %all-to-all-start.5 = ((bf16[4,136,512]{2,1,0:T(8,128)(2,1)}), bf16[4,136,512]{2,1,0:T(8,128)(2,1)S(1)}, u32[]{:S(2)}, u32[]{:S(2)}) async-start(bf16[4,136,512]{2,1,0:T(8,128)(2,1)} %broadcast_in_dim.14), calls=%async_computation.5 | async-start | bytes 1114112 | tf_op jit(solution)/shard_map/all_to_all | solution.py:322
  156.1 6.2 %shard_map.205 = (bf16[352,4096]{1,0:T(8,128)(2,1)}, bf16[352,4096]{1,0:T(8,128)(2,1)}, bf16[352,4096]{1,0:T(8,128)(2,1)}) custom-call(bf16[352,256]{1,0:T(8,128)(2,1)} %fusion.4.own_back, bf16[352,128]{1,0:T(8,128)(2,1)} %fusion.7.routes_back, bf16[256,2048]{1,0:T(8,128)(2,1)} %get-tuple-element.37.slab_query, ...), custom_call_target="tpu_custom_call" | custom-call | flops 1006632960 | bytes 10092544 | tf_op jit(solution)/shard_map/pallas_call | solution.py:372
  162.3 6.2 %shard_map.206 = (bf16[352,4096]{1,0:T(8,128)(2,1)}, bf16[352,4096]{1,0:T(8,128)(2,1)}, bf16[352,4096]{1,0:T(8,128)(2,1)}) custom-call(bf16[352,256]{1,0:T(8,128)(2,1)} %fusion.4.own_back, bf16[352,128]{1,0:T(8,128)(2,1)} %fusion.7.routes_back, ...), custom_call_target="tpu_custom_call", output_to_operand_aliasing={{0}: (7, {}), {1}: (8, {}), {2}: (9, {})} | custom-call | flops 1006632960 | bytes 10092544 | tf_op jit(solution)/shard_map/pallas_call | solution.py:372
  169.2 0.8 copy.37
  (59 shorter events, 6.9 us)
Async XLA Ops:
  6.8 18.8 %all-to-all-start.1 = ((bf16[4,64,2048]{2,1,0:T(8,128)(2,1)}), bf16[4,64,2048]{2,1,0:T(8,128)(2,1)S(1)}, u32[]{:S(2)}, u32[]{:S(2)}) async-start(bf16[4,64,2048]{2,1,0:T(8,128)(2,1)} %shard_map.201), calls=%async_computation.1 | async-start | bytes 2097152 | tf_op jit(solution)/shard_map/all_to_all | solution.py:280
  12.0 4.9 %copy-start.9 = (s32[1,16]{1,0:T(1,128)S(1)}, s32[1,16]{1,0:T(1,128)}, u32[]{:S(2)}) copy-start(s32[1,16]{1,0:T(1,128)} %param.21) | copy-start | bytes 196
  12.0 4.9 %copy-start.8 = (s32[1,256]{1,0:T(1,128)S(1)}, s32[1,256]{1,0:T(1,128)}, u32[]{:S(2)}) copy-start(s32[1,256]{1,0:T(1,128)} %param.20) | copy-start | bytes 3076
  25.6 3.6 %copy-start.2 = (bf16[4,64,2048]{2,1,0:T(8,128)(2,1)}, bf16[4,64,2048]{2,1,0:T(8,128)(2,1)S(1)}, u32[]{:S(2)}) copy-start(bf16[4,64,2048]{2,1,0:T(8,128)(2,1)S(1)} %all-to-all-done.1.arrived) | copy-start | bytes 3145732
  25.6 16.8 %all-to-all-start = ((bf16[4,64,2048]{2,1,0:T(8,128)(2,1)}), bf16[4,64,2048]{2,1,0:T(8,128)(2,1)S(1)}, u32[]{:S(2)}, u32[]{:S(2)}) async-start(bf16[4,64,2048]{2,1,0:T(8,128)(2,1)} %shard_map.199), calls=%async_computation | async-start | bytes 2097152 | tf_op jit(solution)/shard_map/all_to_all | solution.py:280
  29.2 10.1 %copy-start.7 = (f32[128,256]{1,0:T(8,128)S(1)}, f32[128,256]{1,0:T(8,128)}, u32[]{:S(2)}) copy-start(f32[128,256]{1,0:T(8,128)} %constant.69) | copy-start | bytes 393220
  29.2 10.2 %copy-start.6 = (f32[128,256]{1,0:T(8,128)S(1)}, f32[128,256]{1,0:T(8,128)}, u32[]{:S(2)}) copy-start(f32[128,256]{1,0:T(8,128)} %constant.70) | copy-start | bytes 393220
  35.4 5.0 %copy-start.5 = (f32[256,128]{1,0:T(8,128)S(1)}, f32[256,128]{1,0:T(8,128)}, u32[]{:S(2)}) copy-start(f32[256,128]{1,0:T(8,128)} %constant.71) | copy-start | bytes 393220
  35.4 20.9 %collective-permute-start.2 = (bf16[256,2048]{1,0:T(8,128)(2,1)}, bf16[256,2048]{1,0:T(8,128)(2,1)}, u32[]{:S(2)}, u32[]{:S(2)}) collective-permute-start(bf16[256,2048]{1,0:T(8,128)(2,1)} %get-tuple-element.30.right), channel_id=1, source_target_pairs={{0,1},{1,2},{2,3},{3,4},{4,5},{5,6},{6,7},{8,9},{9,10},{10,11},{11... | collective-permute-start | bytes 3145736 | tf_op jit(solution)/shard_map/ppermute | solution.py:297
  37.8 18.5 %collective-permute-start.3 = (bf16[256,2048]{1,0:T(8,128)(2,1)}, bf16[256,2048]{1,0:T(8,128)(2,1)}, u32[]{:S(2)}, u32[]{:S(2)}) collective-permute-start(bf16[256,2048]{1,0:T(8,128)(2,1)} %get-tuple-element.31.left), channel_id=1, source_target_pairs={{1,0},{2,1},{3,2},{4,3},{5,4},{6,5},{7,6},{9,8},{10,9},{11,10},{12... | collective-permute-start | bytes 3145736 | tf_op jit(solution)/shard_map/ppermute | solution.py:298
  39.4 1.7 %copy-start.4 = (f32[256,256]{1,0:T(8,128)S(1)}, f32[256,256]{1,0:T(8,128)}, u32[]{:S(2)}) copy-start(f32[256,256]{1,0:T(8,128)} %constant.68) | copy-start | bytes 786436
  42.4 1.0 copy-start
  49.4 16.4 %collective-permute-start = (bf16[256,2048]{1,0:T(8,128)(2,1)}, bf16[256,2048]{1,0:T(8,128)(2,1)S(1)}, u32[]{:S(2)}, u32[]{:S(2)}) collective-permute-start(bf16[256,2048]{1,0:T(8,128)(2,1)} %get-tuple-element.27.right), channel_id=1, source_target_pairs={{0,1},{1,2},{2,3},{3,4},{4,5},{5,6},{6,7},{8,9},{9,10},{10,11},{11... | collective-permute-start | bytes 3145736 | tf_op jit(solution)/shard_map/ppermute | solution.py:297
  53.4 12.4 %collective-permute-start.1 = (bf16[256,2048]{1,0:T(8,128)(2,1)}, bf16[256,2048]{1,0:T(8,128)(2,1)}, u32[]{:S(2)}, u32[]{:S(2)}) collective-permute-start(bf16[256,2048]{1,0:T(8,128)(2,1)} %get-tuple-element.28.left), channel_id=1, source_target_pairs={{1,0},{2,1},{3,2},{4,3},{5,4},{6,5},{7,6},{9,8},{10,9},{11,10},{12... | collective-permute-start | bytes 3145736 | tf_op jit(solution)/shard_map/ppermute | solution.py:298
  65.8 1.0 copy-start.10
  76.3 20.7 %all-to-all-start.2 = ((bf16[4,64,2048]{2,1,0:T(8,128)(2,1)}), bf16[4,64,2048]{2,1,0:T(8,128)(2,1)S(1)}, u32[]{:S(2)}, u32[]{:S(2)}) async-start(bf16[4,64,2048]{2,1,0:T(8,128)(2,1)} %get-tuple-element.36), calls=%async_computation.2 | async-start | bytes 2097152 | tf_op jit(solution)/shard_map/all_to_all | solution.py:364
  97.0 35.7 %copy-start.1 = (bf16[4,64,2048]{2,1,0:T(8,128)(2,1)}, bf16[4,64,2048]{2,1,0:T(8,128)(2,1)S(1)}, u32[]{:S(2)}) copy-start(bf16[4,64,2048]{2,1,0:T(8,128)(2,1)S(1)} %all-to-all-done.2.arrived) | copy-start | bytes 3145732
  132.7 17.6 %all-to-all-start.3 = ((bf16[4,64,2048]{2,1,0:T(8,128)(2,1)}), bf16[4,64,2048]{2,1,0:T(8,128)(2,1)S(1)}, u32[]{:S(2)}, u32[]{:S(2)}) async-start(bf16[4,64,2048]{2,1,0:T(8,128)(2,1)} %get-tuple-element.39), calls=%async_computation.3 | async-start | bytes 2097152 | tf_op jit(solution)/shard_map/all_to_all | solution.py:364
  150.3 5.8 %copy-start.3 = (bf16[4,64,2048]{2,1,0:T(8,128)(2,1)}, bf16[4,64,2048]{2,1,0:T(8,128)(2,1)S(1)}, u32[]{:S(2)}) copy-start(bf16[4,64,2048]{2,1,0:T(8,128)(2,1)S(1)} %all-to-all-done.3.arrived) | copy-start | bytes 3145732
  151.3 17.3 %all-to-all-start.5 = ((bf16[4,136,512]{2,1,0:T(8,128)(2,1)}), bf16[4,136,512]{2,1,0:T(8,128)(2,1)S(1)}, u32[]{:S(2)}, u32[]{:S(2)}) async-start(bf16[4,136,512]{2,1,0:T(8,128)(2,1)} %broadcast_in_dim.14), calls=%async_computation.5 | async-start | bytes 1114112 | tf_op jit(solution)/shard_map/all_to_all | solution.py:322
